TPU v7x, 512 devices: a whole 4x4x16 slice. The times are simulated.
512 devices in a mesh: row: 8 (over y, core), col: 8 (over x, z_hi), depth: 8 (over z_lo).
Axes of the slice: x: 4, y: 4, z: 16 (z_hi: 2, z_lo: 8; z = z_hi * 8 + z_lo), core: 2. Of those that a mesh axis runs over, the one named last changes fastest.
Arguments:
- layer_input: bfloat16 [4096, 5120], P('depth', 'row'), may hold values from -6 to 6
- output_grad: bfloat16 [4096, 5120], P('depth', 'row'), may hold values from -6 to 6
- w_gate: bfloat16 [5120, 7168], P('row', 'col'), may hold values from -0.078125 to 0.078125
- w_up: bfloat16 [5120, 7168], P('row', 'col'), may hold values from -0.078125 to 0.078125
- w_down: bfloat16 [7168, 5120], P('col', 'row'), may hold values from -0.0625 to 0.0625
Outputs:
- input_grad: float32 [4096, 5120], P('depth', 'row')
- gate_grad: float32 [5120, 7168], P(('row', 'depth'), 'col')
- up_grad: float32 [5120, 7168], P(('row', 'depth'), 'col')
- down_grad: float32 [7168, 5120], P('col', ('row', 'depth'))
All inputs are finite; a program needn't handle non-finite values.
Results may differ from a plain program's by a relative error of at most 0.015.
Values may be sent and summed in bfloat16 or wider, within the bound.
A program may use at most 64 MiB of HBM per device.

v0:
```python
import jax
import jax.numpy as jnp
from jax import lax
from jax.sharding import PartitionSpec as P


def swiglu_back(gate, up, back):
    sig = jax.nn.sigmoid(gate)
    silu = gate * sig
    act = (silu * up).astype(jnp.bfloat16)
    d_gate = (back * up * sig * (1.0 + gate * (1.0 - sig))).astype(jnp.bfloat16)
    d_up = (back * silu).astype(jnp.bfloat16)
    return (d_gate, d_up, act)


def contract_first(left, right):
    return lax.dot_general(
        left, right, (((0,), (0,)), ((), ())), preferred_element_type=jnp.float32
    )


def contract_last(left, right):
    return lax.dot_general(
        left, right, (((1,), (1,)), ((), ())), preferred_element_type=jnp.float32
    )


def shards(layer_input, output_grad, w_gate, w_up, w_down):
    part_gate = jnp.dot(layer_input, w_gate, preferred_element_type=jnp.float32)
    part_up = jnp.dot(layer_input, w_up, preferred_element_type=jnp.float32)
    part_back = contract_last(output_grad, w_down)
    gate, up, back = lax.psum((part_gate, part_up, part_back), "row")
    d_gate, d_up, act = swiglu_back(gate, up, back)
    part_input = contract_last(d_gate, w_gate) + contract_last(d_up, w_up)
    input_grad = lax.psum(part_input, "col")
    factor = float(layer_input.shape[0] * lax.axis_size("depth")) ** (-0.5)
    term_gate = contract_first(layer_input, d_gate) * factor
    term_up = contract_first(layer_input, d_up) * factor
    term_down = contract_first(output_grad, act) * factor
    gate_grad, up_grad, down_grad = (
        lax.psum_scatter(
            term_gate.astype(jnp.bfloat16), "depth", scatter_dimension=0, tiled=True
        ).astype(jnp.float32),
        lax.psum_scatter(
            term_up.astype(jnp.bfloat16), "depth", scatter_dimension=0, tiled=True
        ).astype(jnp.float32),
        lax.psum_scatter(
            term_down.astype(jnp.bfloat16), "depth", scatter_dimension=0, tiled=True
        ).astype(jnp.float32),
    )
    return (input_grad, gate_grad, up_grad, down_grad.T)


def solution(mesh):
    in_specs = (
        P("depth", "row"),
        P("depth", "row"),
        P("row", "col"),
        P("row", "col"),
        P("col", "row"),
    )
    out_specs = (
        P("depth", "row"),
        P(("row", "depth"), "col"),
        P(("row", "depth"), "col"),
        P("col", ("row", "depth")),
    )
    return jax.shard_map(shards, mesh=mesh, in_specs=in_specs, out_specs=out_specs, check_vma=False)
```

profile of v0, /device:TPU:24, one launch (start us, length us, event | category | flops | bytes accessed | tf_op | source)
XLA Modules:
  0.0 591.9 jit_solution(8813124854014182433)
XLA Ops:
  7.2 0.0 copy-start
  7.2 0.0 copy-start.2
  7.2 0.0 copy-start.1
  7.2 0.0 all-reduce.6.cloned.1.call-start
  7.2 1.2 copy-done
  8.4 3.3 fusion.8
  11.7 0.0 copy-done.2
  11.7 0.0 copy-done.1
  11.7 0.0 copy-start.4
  11.7 0.0 copy-start.5
  11.7 2.2 fusion.7
  13.9 0.0 copy-done.4
  13.9 0.0 copy-done.5
  13.9 2.2 fusion.6
  16.2 0.0 all-reduce.6.cloned.1.call-update
  16.2 0.0 reduce-scatter.14.cloned.1.call-start
  16.2 96.8 %all-reduce.6.cloned.1.call-done = (f32[512,896]{1,0:T(8,128)}, f32[512,896]{1,0:T(8,128)}, f32[512,896]{1,0:T(8,128)}) async-done(((f32[512,896]{1,0:T(8,128)}, f32[512,896]{1,0:T(8,128)}, f32[512,896]{1,0:T(8,128)}), (f32[512,896]{1,0:T(8,128)}, f32[512,896]{1,0:T(8,128)}, f32[512,896]{1,0:T(8,128)})) %all-reduce.6.cloned.1.call-update) | async-done | bytes 5505040 | tf_op jit(solution)/shard_map/psum | solution.py:32
  113.0 3.2 fusion.3
  116.2 1.8 copy.19
  118.0 0.0 reduce-scatter.14.cloned.1.call-update
  118.1 0.0 reduce-scatter.12.cloned.1.call-start
  118.1 0.0 copy-start.3
  118.1 4.5 multiply_convert_fusion.4
  122.6 0.0 copy-done.3
  122.6 1.9 fusion.2
  124.5 2.4 copy.17
  126.9 0.0 reduce-scatter.12.cloned.1.call-update
  127.0 0.0 reduce-scatter.10.cloned.1.call-start
  127.0 3.3 fusion.1
  130.3 2.4 copy.15
  132.7 0.0 reduce-scatter.10.cloned.1.call-update
  132.7 0.0 all-reduce.4.cloned.1.call-start
  132.8 2.2 fusion.9
  134.9 2.1 convolution_add_fusion
  137.0 0.0 all-reduce.4.cloned.1.call-update
  137.0 51.5 %reduce-scatter.14.cloned.1.call-done = bf16[80,896]{1,0:T(8,128)(2,1)} async-done(((bf16[640,896]{1,0:T(8,128)(2,1)}), bf16[80,896]{1,0:T(8,128)(2,1)}) %reduce-scatter.14.cloned.1.call-update) | async-done | bytes 143376
  188.5 1.1 copy.20
  189.6 0.9 copy.14
  190.5 62.5 %reduce-scatter.12.cloned.1.call-done = bf16[80,896]{1,0:T(8,128)(2,1)} async-done(((bf16[640,896]{1,0:T(8,128)(2,1)}), bf16[80,896]{1,0:T(8,128)(2,1)}) %reduce-scatter.12.cloned.1.call-update) | async-done | bytes 143376
  253.0 1.1 copy.18
  254.1 0.9 copy.13
  254.9 62.7 %reduce-scatter.10.cloned.1.call-done = bf16[80,896]{1,0:T(8,128)(2,1)} async-done(((bf16[640,896]{1,0:T(8,128)(2,1)}), bf16[80,896]{1,0:T(8,128)(2,1)}) %reduce-scatter.10.cloned.1.call-update) | async-done | bytes 143376
  317.6 1.1 copy.16
  318.7 0.9 copy.12
  319.5 263.3 %all-reduce.4.cloned.1.call-done = f32[512,640]{1,0:T(8,128)} async-done(((f32[512,640]{1,0:T(8,128)}), f32[512,640]{1,0:T(8,128)}) %all-reduce.4.cloned.1.call-update) | async-done | bytes 1310736 | tf_op jit(solution)/shard_map/psum | solution.py:35
  582.9 2.5 copy.25
  (1 shorter events, 0.0 us)
Async XLA Ops:
  7.2 1.3 copy-start
  7.2 4.5 copy-start.2
  7.2 4.5 copy-start.1
  7.2 105.8 %all-reduce.6.cloned.1.call-start = ((), (), s32[]{:S(2)}) async-start(), calls=%async_computation.7 | async-start | bytes 11010048 | tf_op jit(solution)/shard_map/psum | solution.py:32
  11.7 2.2 copy-start.4
  11.7 2.2 copy-start.5
  16.2 172.3 %reduce-scatter.14.cloned.1.call-start = ((), (), s32[]{:S(2)}) async-start(), calls=%async_computation.6 | async-start | bytes 1290240
  118.1 134.9 %reduce-scatter.12.cloned.1.call-start = ((), (), s32[]{:S(2)}) async-start(), calls=%async_computation.5 | async-start | bytes 1290240
  118.1 4.5 copy-start.3
  127.0 190.7 %reduce-scatter.10.cloned.1.call-start = ((), (), s32[]{:S(2)}) async-start(), calls=%async_computation.4 | async-start | bytes 1290240
  132.7 450.2 %all-reduce.4.cloned.1.call-start = ((), (), s32[]{:S(2)}) async-start(), calls=%async_computation.3 | async-start | bytes 2621440 | tf_op jit(solution)/shard_map/psum | solution.py:35
Sparse Core Ops, SparseCore 0:
  16.3 96.7 all-reduce.5
  118.2 70.2 reduce-scatter.13
  191.3 61.6 reduce-scatter.11
  255.7 61.8 reduce-scatter.9
  321.0 261.8 all-reduce.3
where the time goes:
time: 594 us; the launch traced here: 592 us
  waiting for transfers between devices  537 us (90%)
  matrix products  20.3 us (3%)
  local copies, waits for them, and re-layouts  16.1 us (3%)
  between operations  13.9 us (2%)
    psum x1, waiting for transfers between devices, shards(): input_grad = lax.psum(part_input, 'col')  263 us
    unnamed x8, waiting for transfers between devices  177 us
    psum x1, waiting for transfers between devices, shards(): gate, up, back = lax.psum((part_gate, part_up, part_back), 'row')  96.8 us
    unnamed x22, local copies, waits for them, and re-layouts  16.1 us
  transfers between devices with their start and end apart: 5, of which 5 were waited for; matrix products, arithmetic and copies ran while one was open for 4% of the time, Pallas kernels for 0%

commit v1 on v0

v1 whole, which is shorter than its diff:
```python
import jax
import jax.numpy as jnp
from jax import lax
from jax.experimental import pallas as pl
from jax.experimental.pallas import tpu as pltpu
from jax.sharding import PartitionSpec as P

MESH = pl.DeviceIdType.MESH
BF, F32 = jnp.bfloat16, jnp.float32

NY, NX, NZ = 4, 4, 8
TOK, FEAT, HID = 512, 640, 896
HALF = TOK // 2
QUART = HALF // NY
XTOK = TOK // NX
CHUNK = FEAT // NZ
ROWS = 3 * CHUNK
LANE = 128
UNITS = HID // LANE
SLICES = ((0, 256), (256, 256), (512, 256), (768, 128))
NS = len(SLICES)
HOPS = NZ - 1
STEPS = UNITS * HOPS
SKEW = 4


def swiglu_back(gate, up, back):
    sig = jax.nn.sigmoid(gate)
    silu = gate * sig
    d_gate = (back * up * sig * (1.0 + gate * (1.0 - sig))).astype(BF)
    return d_gate, (back * silu).astype(BF), (silu * up).astype(BF)


def dot(a, b):
    return jnp.dot(a, b, preferred_element_type=F32)


def dot_last(a, b):
    return lax.dot_general(a, b, (((1,), (1,)), ((), ())), preferred_element_type=F32)


def kernel(factor, x_ref, g_ref, wg_ref, wu_ref, wd_ref, ig_ref, wgr_ref, *scratch):
    it = iter(scratch)
    xt = next(it)
    ph = [next(it) for _ in SLICES]
    csend = [next(it) for _ in SLICES]
    crecv = [next(it) for _ in SLICES]
    ysend = [next(it) for _ in SLICES]
    yrecv = [next(it) for _ in SLICES]
    dbuf = [next(it) for _ in SLICES]
    zterm, zl, zr = next(it), next(it), next(it)
    ig, xsend, xrecv, hsend, hrecv, agbuf = (next(it) for _ in range(6))
    cs, cr, ys, yr, gs, gr, fs, fr, zs, zlr, zrr, xs, xr, hs, hr, ags, agr = it

    row, col, dep = lax.axis_index("row"), lax.axis_index("col"), lax.axis_index("depth")
    y, k = row // 2, row % 2
    x, zh = col // 2, col % 2
    other = (y * 2 + 1 - k, col, dep)

    def at_y(o):
        return (((y + o) % NY) * 2 + k, col, dep)

    def at_x(o):
        return (row, ((x + o) % NX) * 2 + zh, dep)

    partner = (row, x * 2 + 1 - zh, dep)
    up_z = (row, col, dep + 1)
    down_z = (row, col, dep - 1)

    barrier = pltpu.get_barrier_semaphore()

    def greet(dev):
        pl.semaphore_signal(barrier, inc=1, device_id=dev, device_id_type=MESH)

    for o in (1, 2, 3):
        greet(at_y(o))
        greet(at_x(o))
    greet(other)
    greet(partner)

    @pl.when(dep > 0)
    def _():
        greet(down_z)

    @pl.when(dep < NZ - 1)
    def _():
        greet(up_z)

    def copy(src, dst, ssem, rsem, dev):
        return pltpu.make_async_remote_copy(
            src_ref=src, dst_ref=dst, send_sem=ssem, recv_sem=rsem, device_id=dev, device_id_type=MESH
        )

    def partials(half, s):
        lo, w = SLICES[s]
        rows = pl.ds(pl.multiple_of(half * HALF, HALF), HALF)
        return (
            dot(x_ref[rows, :], wg_ref[:, lo:lo + w]),
            dot(x_ref[rows, :], wu_ref[:, lo:lo + w]),
            dot_last(g_ref[rows, :], wd_ref[lo:lo + w, :]),
        )

    def core_copy(s):
        return copy(csend[s], crecv[s], cs.at[s], cr.at[s], other)

    def first(s):
        for m, part in enumerate(partials(1 - k, s)):
            csend[s][m] = part.astype(BF)
        if s == 0:
            inner = jnp.where((dep > 0) & (dep < NZ - 1), 10, 9)
            pl.semaphore_wait(barrier, inner)
        core_copy(s).start()
        for m, part in enumerate(partials(k, s)):
            ph[s][m] = part

    def y_copy(s, o):
        return copy(ysend[s].at[(y + o) % NY], yrecv[s].at[o - 1], ys.at[s, o - 1], yr.at[s, o - 1], at_y(o))

    def reduce_core(s):
        core_copy(s).wait_recv()
        for m in range(3):
            total = ph[s][m] + crecv[s][m].astype(F32)
            ph[s][m] = total
            for b in range(NY):
                ysend[s][b, m] = total[b * QUART:(b + 1) * QUART].astype(BF)
        for o in (2, 1, 3):
            y_copy(s, o).start()

    def gather_copy(s, o):
        blk = k * NY + y
        return copy(dbuf[s].at[blk], dbuf[s].at[blk], gs.at[s, o - 1], gr.at[s, o - 1], at_y(o))

    def cross_copy(s, o):
        blk = k * NY + (y - o + NY) % NY
        return copy(dbuf[s].at[blk], dbuf[s].at[blk], fs.at[s, o], fr.at[s, o], other)

    def middle(s):
        for o in (1, 2, 3):
            y_copy(s, o).wait_recv()
        own = pl.ds(pl.multiple_of(y * QUART, QUART), QUART)
        sums = []
        for m in range(3):
            total = ph[s][m, own, :]
            for o in range(3):
                total = total + yrecv[s][o, m].astype(F32)
            sums.append(total)
        blk = k * NY + y
        for m, value in enumerate(swiglu_back(*sums)):
            dbuf[s][blk, m] = value
        for o in (2, 1, 3):
            gather_copy(s, o).start()
        cross_copy(s, 0).start()

    def spread(s):
        for o in (1, 3, 2):
            gather_copy(s, o).wait_recv()
            cross_copy(s, o).start()

    def arrive(s):
        for o in range(NY):
            cross_copy(s, o).wait_recv()

    def hidden(s, m):
        return dbuf[s][:, m].reshape(TOK, SLICES[s][1])

    def inputs(s):
        lo, w = SLICES[s]
        part = dot_last(hidden(s, 0), wg_ref[:, lo:lo + w]) + dot_last(hidden(s, 1), wu_ref[:, lo:lo + w])
        if s == 0:
            ig[...] = part
        elif s < NS - 1:
            ig[...] += part
        else:
            total = ig[...] + part
            ig[...] = total
            for b in range(NX):
                xsend[b] = total[b * XTOK:(b + 1) * XTOK].astype(BF)

    def weights(s):
        lo, w = SLICES[s]
        for m in range(3):
            term = (dot(xt[m // 2], hidden(s, m)) * factor).astype(BF)
            for v in range(w // LANE):
                for j in range(NZ):
                    zterm[lo // LANE + v, j, m * CHUNK:(m + 1) * CHUNK, :] = term[
                        j * CHUNK:(j + 1) * CHUNK, v * LANE:(v + 1) * LANE
                    ]

    def z_up(u, j):
        return copy(zterm.at[u, j], zl.at[u, j], zs.at[u, j], zlr.at[u, j], up_z)

    def z_down(u, j):
        return copy(zterm.at[u, j], zr.at[u, j], zs.at[u, j], zrr.at[u, j], down_z)

    def z_step(t, carry):
        q = t - SKEW * dep
        qc = jnp.clip(q, 0, STEPS - 1)
        u, j = qc // HOPS, HOPS - qc % HOPS

        @pl.when((q >= 0) & (q < STEPS) & (j > dep))
        def _():
            @pl.when(dep > 0)
            def _():
                z_up(u, j).wait_recv()
                zterm[u, j] = (zterm[u, j].astype(F32) + zl[u, j].astype(F32)).astype(BF)

            z_up(u, j).start()

        p = t - SKEW * (NZ - 1 - dep)
        pc = jnp.clip(p, 0, STEPS - 1)
        v, i = pc // HOPS, pc % HOPS

        @pl.when((p >= 0) & (p < STEPS) & (i < dep))
        def _():
            @pl.when(dep < NZ - 1)
            def _():
                z_down(v, i).wait_recv()
                zterm[v, i] = (zterm[v, i].astype(F32) + zr[v, i].astype(F32)).astype(BF)

            z_down(v, i).start()

        return carry

    def z_steps(lo, hi):
        lax.fori_loop(lo, hi, z_step, 0)

    def x_copy(o):
        return copy(xsend.at[(x + o) % NX], xrecv.at[o - 1], xs.at[o - 1], xr.at[o - 1], at_x(o))

    def hi_copy():
        return copy(hsend, hrecv, hs.at[0], hr.at[0], partner)

    def ag_copy(o):
        return copy(agbuf.at[x], agbuf.at[x], ags.at[o - 1], agr.at[o - 1], at_x(o))

    def units_of(s):
        lo, w = SLICES[s]
        return lo // LANE * HOPS, (lo + w) // LANE * HOPS

    for s in range(NS):
        first(s)
        if s > 0:
            reduce_core(s - 1)
    reduce_core(NS - 1)
    xt[0] = x_ref[...].T
    xt[1] = g_ref[...].T
    middle(0)
    middle(1)
    spread(0)
    middle(2)
    spread(1)
    arrive(0)
    inputs(0)
    weights(0)
    z_steps(*units_of(0))
    middle(3)
    spread(2)
    arrive(1)
    inputs(1)
    weights(1)
    z_steps(*units_of(1))
    spread(3)
    arrive(2)
    inputs(2)
    weights(2)
    z_steps(units_of(2)[0], units_of(2)[0] + HOPS)
    arrive(3)
    inputs(3)
    for o in (2, 1, 3):
        x_copy(o).start()
    weights(3)
    z_steps(units_of(2)[0] + HOPS, units_of(3)[0])
    for o in (1, 3, 2):
        x_copy(o).wait_recv()
    mine = pl.ds(pl.multiple_of(x * XTOK, XTOK), XTOK)
    total = ig[mine, :]
    for o in range(3):
        total = total + xrecv[o].astype(F32)
    hsend[...] = total.astype(BF)
    hi_copy().start()
    z_steps(units_of(3)[0], STEPS + SKEW * 2)
    hi_copy().wait_recv()
    agbuf[x] = (hsend[...].astype(F32) + hrecv[...].astype(F32)).astype(BF)
    for o in (2, 1, 3):
        ag_copy(o).start()
    z_steps(STEPS + SKEW * 2, STEPS + SKEW * (NZ - 1))

    def finish(u, carry):
        @pl.when(dep > 0)
        def _():
            z_up(u, dep).wait_recv()

        @pl.when(dep < NZ - 1)
        def _():
            z_down(u, dep).wait_recv()

        lanes = pl.ds(pl.multiple_of(u * LANE, LANE), LANE)
        wgr_ref[:, lanes] = zterm[u, dep].astype(F32)

        @pl.when(dep > 0)
        def _():
            wgr_ref[:, lanes] += zl[u, dep].astype(F32)

        @pl.when(dep < NZ - 1)
        def _():
            wgr_ref[:, lanes] += zr[u, dep].astype(F32)

        return carry

    lax.fori_loop(0, UNITS, finish, 0)

    for o in (1, 3, 2):
        ag_copy(o).wait_recv()
    ig_ref[...] = agbuf[...].reshape(TOK, FEAT)

    for s in range(NS):
        core_copy(s).wait_send()
        for o in (1, 2, 3):
            y_copy(s, o).wait_send()
            gather_copy(s, o).wait_send()
        for o in range(NY):
            cross_copy(s, o).wait_send()
    for o in (1, 2, 3):
        x_copy(o).wait_send()
        ag_copy(o).wait_send()
    hi_copy().wait_send()

    def drain(q, carry):
        u, j = q // NZ, q % NZ

        @pl.when(j != dep)
        def _():
            z_up(u, j).wait_send()

        return carry

    lax.fori_loop(0, UNITS * NZ, drain, 0)


def shards(layer_input, output_grad, w_gate, w_up, w_down):
    factor = float(layer_input.shape[0] * lax.axis_size("depth")) ** (-0.5)
    dma = pltpu.SemaphoreType.DMA

    def per_slice(lead, dtype):
        return [pltpu.VMEM((*lead, w), dtype) for _, w in SLICES]

    scratch = [
        pltpu.VMEM((2, FEAT, TOK), BF),
        *per_slice((3, HALF), F32),
        *per_slice((3, HALF), BF),
        *per_slice((3, HALF), BF),
        *per_slice((NY, 3, QUART), BF),
        *per_slice((NY - 1, 3, QUART), BF),
        *per_slice((2 * NY, 3, QUART), BF),
        pltpu.VMEM((UNITS, NZ, ROWS, LANE), BF),
        pltpu.VMEM((UNITS, NZ, ROWS, LANE), BF),
        pltpu.VMEM((UNITS, NZ, ROWS, LANE), BF),
        pltpu.VMEM((TOK, FEAT), F32),
        pltpu.VMEM((NX, XTOK, FEAT), BF),
        pltpu.VMEM((NX - 1, XTOK, FEAT), BF),
        pltpu.VMEM((XTOK, FEAT), BF),
        pltpu.VMEM((XTOK, FEAT), BF),
        pltpu.VMEM((NX, XTOK, FEAT), BF),
        dma((NS,)), dma((NS,)),
        dma((NS, 3)), dma((NS, 3)),
        dma((NS, 3)), dma((NS, 3)),
        dma((NS, NY)), dma((NS, NY)),
        dma((UNITS, NZ)), dma((UNITS, NZ)), dma((UNITS, NZ)),
        dma((3,)), dma((3,)),
        dma((1,)), dma((1,)),
        dma((3,)), dma((3,)),
    ]
    vmem = pl.BlockSpec(memory_space=pltpu.VMEM)
    ig, wgr = pl.pallas_call(
        lambda *refs: kernel(factor, *refs),
        out_shape=(
            jax.ShapeDtypeStruct((TOK, FEAT), BF),
            jax.ShapeDtypeStruct((ROWS, HID), F32),
        ),
        in_specs=[vmem] * 5,
        out_specs=(vmem, vmem),
        scratch_shapes=scratch,
        compiler_params=pltpu.CompilerParams(
            collective_id=0, has_side_effects=True, vmem_limit_bytes=56 * 2 ** 20
        ),
        name="swiglu_back",
    )(layer_input, output_grad, w_gate, w_up, w_down)
    return ig.astype(F32), wgr[:CHUNK], wgr[CHUNK:2 * CHUNK], wgr[2 * CHUNK:].T


def solution(mesh):
    in_specs = (
        P("depth", "row"),
        P("depth", "row"),
        P("row", "col"),
        P("row", "col"),
        P("col", "row"),
    )
    out_specs = (
        P("depth", "row"),
        P(("row", "depth"), "col"),
        P(("row", "depth"), "col"),
        P("col", ("row", "depth")),
    )
    return jax.shard_map(shards, mesh=mesh, in_specs=in_specs, out_specs=out_specs, check_vma=False)
```

time: 594 us -> 150 us (0.25)
  waiting for transfers between devices: 537 us -> 0 us
  Pallas kernels: 0 us -> 143 us
  matrix products: 20.3 us -> 0 us
  local copies, waits for them, and re-layouts: 16.1 us -> 2.12 us
  between operations: 13.9 us -> 0.65 us
    psum x2 -> x0, waiting for transfers between devices: 360 us -> none  [the longest x1 263 us: shards(): input_grad = lax.psum(part_input, 'col')]
    unnamed x8 -> x0, waiting for transfers between devices: 177 us -> none
    pallas_call x0 -> x1, Pallas kernels: none -> 143 us  [shards(): pl.pallas_call(lambda *refs: kernel(factor, *refs), out_shape=(jax.ShapeD...]
    dot_general x8 -> x0, matrix products: 20.3 us -> none  [the longest x3 8.36 us: contract_first(): lax.dot_general(left, right, (((0,), (0,)), ((), ())), preferred_element_...]
    unnamed x22 -> x2, local copies, waits for them, and re-layouts: 16.1 us -> 0.01 us
  transfers between devices with their start and end apart: 5 -> 0, of which waited for: 5 -> 0; matrix products, arithmetic and copies ran while one was open for 4% -> 0% of each run, Pallas kernels for 0% -> 0%
where the time goes in v1:
time: 150 us; the launch traced here: 147 us
  Pallas kernels  143 us (95%)
  local copies, waits for them, and re-layouts  2.12 us (1%)
    pallas_call x1, Pallas kernels, shards(): pl.pallas_call(lambda *refs: kernel(factor, *refs), out_shape=(jax.ShapeD...  143 us

profile of v1, /device:TPU:24, one launch (start us, length us, event | category | flops | bytes accessed | tf_op | source)
XLA Modules:
  0.0 147.4 jit_solution(8055780724439099746)
XLA Ops:
  0.6 143.4 %swiglu_back.1 = (bf16[512,640]{1,0:T(8,128)(2,1)}, f32[240,896]{1,0:T(8,128)}) custom-call(bf16[512,640]{1,0:T(8,128)(2,1)} %refs_0_.1, bf16[512,640]{1,0:T(8,128)(2,1)} %refs_1_.1, bf16[640,896]{1,0:T(8,128)(2,1)} %refs_2_.1, bf16[640,896]{1,0:T(8,128)(2,1)} %refs_3_.1, bf16[896,640]{1,0:T(8,128)(2,1)} %refs_4_.1), custom_call_target="tpu_custom_call" | custom-call | tf_op jit(solution)/shard_map/swiglu_back/pallas_call | solution.py:374
  144.1 0.0 copy-start
  144.1 2.1 %slice_bitcast_fusion = (f32[896,80]{0,1:T(8,128)}, f32[80,896]{1,0:T(8,128)}, f32[80,896]{1,0:T(8,128)}) fusion(f32[240,896]{1,0:T(8,128)} %get-tuple-element.7), kind=kLoop, calls=%fused_computation | loop fusion | bytes 1720320 | tf_op jit(solution)/shard_map/transpose | solution.py:388
  146.2 0.0 copy-done
  146.2 1.1 convert_element_type.3
Async XLA Ops:
  144.1 2.1 %copy-start = (bf16[512,640]{1,0:T(8,128)(2,1)S(1)}, bf16[512,640]{1,0:T(8,128)(2,1)}, u32[]{:S(2)}) copy-start(bf16[512,640]{1,0:T(8,128)(2,1)} %get-tuple-element.6) | copy-start | bytes 1966084

commit v2 on v1

--- a/solution.py
+++ b/solution.py
@@ -17,11 +17,14 @@
 ROWS = 3 * CHUNK
 LANE = 128
 UNITS = HID // LANE
-SLICES = ((0, 256), (256, 256), (512, 256), (768, 128))
+SLICES = ((0, 128), (128, 256), (384, 256), (640, 256))
 NS = len(SLICES)
 HOPS = NZ - 1
 STEPS = UNITS * HOPS
+EARLY = 3
+LATE = UNITS - EARLY
 SKEW = 4
+LAST = STEPS + SKEW * (NZ - 3)
 
 
 def swiglu_back(gate, up, back):
@@ -39,8 +42,17 @@
     return lax.dot_general(a, b, (((1,), (1,)), ((), ())), preferred_element_type=F32)
 
 
-def kernel(factor, x_ref, g_ref, wg_ref, wu_ref, wd_ref, ig_ref, wgr_ref, *scratch):
+def kernel(factor, x_in, g_in, wg_in, wu_in, wd_in, ig_ref, wgr_ref, *scratch):
     it = iter(scratch)
+    x_ref, g_ref, wg_ref, wu_ref, wd_ref, loads, ring = (next(it) for _ in range(7))
+    load = [
+        pltpu.make_async_copy(src, dst, loads.at[n])
+        for n, (src, dst) in enumerate(
+            ((x_in, x_ref), (wg_in, wg_ref), (wu_in, wu_ref), (g_in, g_ref), (wd_in, wd_ref))
+        )
+    ]
+    for c in load:
+        c.start()
     xt = next(it)
     ph = [next(it) for _ in SLICES]
     csend = [next(it) for _ in SLICES]
@@ -64,53 +76,52 @@
         return (row, ((x + o) % NX) * 2 + zh, dep)
 
     partner = (row, x * 2 + 1 - zh, dep)
-    up_z = (row, col, dep + 1)
-    down_z = (row, col, dep - 1)
+    up_z = (row, x * 2 + (zh + (dep + 1) // NZ) % 2, (dep + 1) % NZ)
+    down_z = (row, x * 2 + (zh + 1 - (dep + NZ - 1) // NZ) % 2, (dep + NZ - 1) % NZ)
 
     barrier = pltpu.get_barrier_semaphore()
-
-    def greet(dev):
+    near = [at_y(1), at_y(2), at_y(3), at_x(1), at_x(2), at_x(3), other, up_z, down_z]
+    for dev in near:
         pl.semaphore_signal(barrier, inc=1, device_id=dev, device_id_type=MESH)
 
-    for o in (1, 2, 3):
-        greet(at_y(o))
-        greet(at_x(o))
-    greet(other)
-    greet(partner)
-
-    @pl.when(dep > 0)
-    def _():
-        greet(down_z)
-
-    @pl.when(dep < NZ - 1)
-    def _():
-        greet(up_z)
+    def tell():
+        pl.semaphore_signal(ring, inc=1, device_id=up_z, device_id_type=MESH)
+
+    def pass_on():
+        pl.semaphore_wait(ring, 1)
+        tell()
 
     def copy(src, dst, ssem, rsem, dev):
         return pltpu.make_async_remote_copy(
             src_ref=src, dst_ref=dst, send_sem=ssem, recv_sem=rsem, device_id=dev, device_id_type=MESH
         )
 
-    def partials(half, s):
+    def partials(half, s, loaded):
         lo, w = SLICES[s]
         rows = pl.ds(pl.multiple_of(half * HALF, HALF), HALF)
-        return (
-            dot(x_ref[rows, :], wg_ref[:, lo:lo + w]),
-            dot(x_ref[rows, :], wu_ref[:, lo:lo + w]),
-            dot_last(g_ref[rows, :], wd_ref[lo:lo + w, :]),
-        )
+        if not loaded:
+            load[0].wait()
+            load[1].wait()
+        yield dot(x_ref[rows, :], wg_ref[:, lo:lo + w])
+        if not loaded:
+            load[2].wait()
+        yield dot(x_ref[rows, :], wu_ref[:, lo:lo + w])
+        if not loaded:
+            load[3].wait()
+            load[4].wait()
+        yield dot_last(g_ref[rows, :], wd_ref[lo:lo + w, :])
 
     def core_copy(s):
         return copy(csend[s], crecv[s], cs.at[s], cr.at[s], other)
 
     def first(s):
-        for m, part in enumerate(partials(1 - k, s)):
+        for m, part in enumerate(partials(1 - k, s, s > 0)):
             csend[s][m] = part.astype(BF)
         if s == 0:
-            inner = jnp.where((dep > 0) & (dep < NZ - 1), 10, 9)
-            pl.semaphore_wait(barrier, inner)
+            pl.semaphore_wait(barrier, len(near))
+            tell()
         core_copy(s).start()
-        for m, part in enumerate(partials(k, s)):
+        for m, part in enumerate(partials(k, s, True)):
             ph[s][m] = part
 
     def y_copy(s, o):
@@ -192,31 +203,45 @@
     def z_down(u, j):
         return copy(zterm.at[u, j], zr.at[u, j], zs.at[u, j], zrr.at[u, j], down_z)
 
+    def place(q):
+        late = q - EARLY * HOPS
+        u = jnp.where(late < 0, q // HOPS, EARLY + late % LATE)
+        return u, jnp.where(late < 0, q % HOPS, late // LATE)
+
+    def z_first(lo, hi):
+        def send(q, carry):
+            u, j = place(q)
+
+            @pl.when(dep == 0)
+            def _():
+                z_up(u, HOPS - j).start()
+
+            @pl.when(dep == NZ - 1)
+            def _():
+                z_down(u, j).start()
+
+            return carry
+
+        lax.fori_loop(lo * HOPS, hi * HOPS, send, 0)
+
     def z_step(t, carry):
-        q = t - SKEW * dep
-        qc = jnp.clip(q, 0, STEPS - 1)
-        u, j = qc // HOPS, HOPS - qc % HOPS
-
-        @pl.when((q >= 0) & (q < STEPS) & (j > dep))
-        def _():
-            @pl.when(dep > 0)
-            def _():
-                z_up(u, j).wait_recv()
-                zterm[u, j] = (zterm[u, j].astype(F32) + zl[u, j].astype(F32)).astype(BF)
-
+        q = t - SKEW * (dep - 1)
+        u, j = place(jnp.clip(q, 0, STEPS - 1))
+        j = HOPS - j
+
+        @pl.when((q >= 0) & (q < STEPS) & (j > dep) & (dep > 0))
+        def _():
+            z_up(u, j).wait_recv()
+            zterm[u, j] = (zterm[u, j].astype(F32) + zl[u, j].astype(F32)).astype(BF)
             z_up(u, j).start()
 
-        p = t - SKEW * (NZ - 1 - dep)
-        pc = jnp.clip(p, 0, STEPS - 1)
-        v, i = pc // HOPS, pc % HOPS
-
-        @pl.when((p >= 0) & (p < STEPS) & (i < dep))
-        def _():
-            @pl.when(dep < NZ - 1)
-            def _():
-                z_down(v, i).wait_recv()
-                zterm[v, i] = (zterm[v, i].astype(F32) + zr[v, i].astype(F32)).astype(BF)
-
+        p = t - SKEW * (NZ - 2 - dep)
+        v, i = place(jnp.clip(p, 0, STEPS - 1))
+
+        @pl.when((p >= 0) & (p < STEPS) & (i < dep) & (dep < NZ - 1))
+        def _():
+            z_down(v, i).wait_recv()
+            zterm[v, i] = (zterm[v, i].astype(F32) + zr[v, i].astype(F32)).astype(BF)
             z_down(v, i).start()
 
         return carry
@@ -233,43 +258,52 @@
     def ag_copy(o):
         return copy(agbuf.at[x], agbuf.at[x], ags.at[o - 1], agr.at[o - 1], at_x(o))
 
-    def units_of(s):
-        lo, w = SLICES[s]
-        return lo // LANE * HOPS, (lo + w) // LANE * HOPS
-
-    for s in range(NS):
-        first(s)
-        if s > 0:
-            reduce_core(s - 1)
-    reduce_core(NS - 1)
+    first(0)
+    first(1)
+    reduce_core(0)
     xt[0] = x_ref[...].T
     xt[1] = g_ref[...].T
+    pass_on()
+    first(2)
     middle(0)
+    reduce_core(1)
+    pass_on()
+    first(3)
+    reduce_core(2)
+    spread(0)
+    arrive(0)
+    weights(0)
+    z_first(0, 1)
+    pass_on()
     middle(1)
-    spread(0)
+    reduce_core(3)
+    inputs(0)
+    pass_on()
+    spread(1)
+    arrive(1)
+    weights(1)
+    z_first(1, EARLY)
+    pass_on()
     middle(2)
-    spread(1)
-    arrive(0)
-    inputs(0)
-    weights(0)
-    z_steps(*units_of(0))
+    inputs(1)
+    z_steps(0, 4)
+    pass_on()
     middle(3)
+    z_steps(4, 7)
     spread(2)
-    arrive(1)
-    inputs(1)
-    weights(1)
-    z_steps(*units_of(1))
-    spread(3)
     arrive(2)
     inputs(2)
-    weights(2)
-    z_steps(units_of(2)[0], units_of(2)[0] + HOPS)
+    pass_on()
+    z_steps(7, 10)
+    spread(3)
     arrive(3)
     inputs(3)
     for o in (2, 1, 3):
         x_copy(o).start()
+    weights(2)
     weights(3)
-    z_steps(units_of(2)[0] + HOPS, units_of(3)[0])
+    z_first(EARLY, UNITS)
+    z_steps(10, 20)
     for o in (1, 3, 2):
         x_copy(o).wait_recv()
     mine = pl.ds(pl.multiple_of(x * XTOK, XTOK), XTOK)
@@ -277,13 +311,14 @@
     for o in range(3):
         total = total + xrecv[o].astype(F32)
     hsend[...] = total.astype(BF)
+    pl.semaphore_wait(ring, 1)
     hi_copy().start()
-    z_steps(units_of(3)[0], STEPS + SKEW * 2)
+    z_steps(20, 36)
     hi_copy().wait_recv()
     agbuf[x] = (hsend[...].astype(F32) + hrecv[...].astype(F32)).astype(BF)
     for o in (2, 1, 3):
         ag_copy(o).start()
-    z_steps(STEPS + SKEW * 2, STEPS + SKEW * (NZ - 1))
+    z_steps(36, LAST)
 
     def finish(u, carry):
         @pl.when(dep > 0)
@@ -345,6 +380,13 @@
         return [pltpu.VMEM((*lead, w), dtype) for _, w in SLICES]
 
     scratch = [
+        pltpu.VMEM((TOK, FEAT), BF),
+        pltpu.VMEM((TOK, FEAT), BF),
+        pltpu.VMEM((FEAT, HID), BF),
+        pltpu.VMEM((FEAT, HID), BF),
+        pltpu.VMEM((HID, FEAT), BF),
+        dma((5,)),
+        pltpu.SemaphoreType.REGULAR,
         pltpu.VMEM((2, FEAT, TOK), BF),
         *per_slice((3, HALF), F32),
         *per_slice((3, HALF), BF),
@@ -377,7 +419,7 @@
             jax.ShapeDtypeStruct((TOK, FEAT), BF),
             jax.ShapeDtypeStruct((ROWS, HID), F32),
         ),
-        in_specs=[vmem] * 5,
+        in_specs=[pl.BlockSpec(memory_space=pl.ANY)] * 5,
         out_specs=(vmem, vmem),
         scratch_shapes=scratch,
         compiler_params=pltpu.CompilerParams(

time: 150 us -> 134 us (0.89)
  Pallas kernels: 143 us -> 129 us
    pallas_call x1, Pallas kernels: 143 us -> 129 us  [shards(): pl.pallas_call(lambda *refs: kernel(factor, *refs), out_shape=(jax.ShapeD...]
where the time goes in v2:
time: 134 us; the launch traced here: 133 us
  Pallas kernels  129 us (96%)
  local copies, waits for them, and re-layouts  2.12 us (2%)
    pallas_call x1, Pallas kernels, shards(): pl.pallas_call(lambda *refs: kernel(factor, *refs), out_shape=(jax.ShapeD...  129 us

profile of v2, /device:TPU:24, one launch (start us, length us, event | category | flops | bytes accessed | tf_op | source)
XLA Modules:
  0.0 132.7 jit_solution(222493820566413044)
XLA Ops:
  0.6 128.8 %swiglu_back.1 = (bf16[512,640]{1,0:T(8,128)(2,1)}, f32[240,896]{1,0:T(8,128)}) custom-call(bf16[512,640]{1,0:T(8,128)(2,1)} %refs_0_.1, bf16[512,640]{1,0:T(8,128)(2,1)} %refs_1_.1, bf16[640,896]{1,0:T(8,128)(2,1)} %refs_2_.1, bf16[640,896]{1,0:T(8,128)(2,1)} %refs_3_.1, bf16[896,640]{1,0:T(8,128)(2,1)} %refs_4_.1), custom_call_target="tpu_custom_call" | custom-call | tf_op jit(solution)/shard_map/swiglu_back/pallas_call | solution.py:416
  129.4 0.0 copy-start
  129.4 2.1 %slice_bitcast_fusion = (f32[896,80]{0,1:T(8,128)}, f32[80,896]{1,0:T(8,128)}, f32[80,896]{1,0:T(8,128)}) fusion(f32[240,896]{1,0:T(8,128)} %get-tuple-element.7), kind=kLoop, calls=%fused_computation | loop fusion | bytes 1720320 | tf_op jit(solution)/shard_map/transpose | solution.py:430
  131.5 0.0 copy-done
  131.5 1.1 convert_element_type.3
Async XLA Ops:
  129.4 2.1 %copy-start = (bf16[512,640]{1,0:T(8,128)(2,1)S(1)}, bf16[512,640]{1,0:T(8,128)(2,1)}, u32[]{:S(2)}) copy-start(bf16[512,640]{1,0:T(8,128)(2,1)} %get-tuple-element.6) | copy-start | bytes 1966084

commit v3 on v2

--- a/solution.py
+++ b/solution.py
@@ -17,14 +17,21 @@
 ROWS = 3 * CHUNK
 LANE = 128
 UNITS = HID // LANE
-SLICES = ((0, 128), (128, 256), (384, 256), (640, 256))
+SLICES = ((0, 128), (128, 128), (256, 256), (512, 384))
 NS = len(SLICES)
 HOPS = NZ - 1
-STEPS = UNITS * HOPS
-EARLY = 3
+EARLY = 4
 LATE = UNITS - EARLY
+MOVED = (3,)
+NM = len(MOVED)
 SKEW = 4
-LAST = STEPS + SKEW * (NZ - 3)
+FAR = HOPS - 2
+FIRST = HOPS
+SECOND = FIRST + FAR
+THIRD = SECOND + (EARLY - 2) * FAR
+NEAR_STEPS = EARLY * HOPS
+FAR_STEPS = THIRD + LATE * FAR
+LAST = THIRD + max(LATE * (HOPS - d) + SKEW * (d - 1) for d in range(2, HOPS))
 
 
 def swiglu_back(gate, up, back):
@@ -62,7 +69,10 @@
     dbuf = [next(it) for _ in SLICES]
     zterm, zl, zr = next(it), next(it), next(it)
     ig, xsend, xrecv, hsend, hrecv, agbuf = (next(it) for _ in range(6))
-    cs, cr, ys, yr, gs, gr, fs, fr, zs, zlr, zrr, xs, xr, hs, hr, ags, agr = it
+    ownq, fq, xt2, fsum = next(it), next(it), next(it), next(it)
+    fd = [next(it) for _ in MOVED]
+    cs, cr, ys, yr, gs, gr, fs, fr, zs, zlr, zrr, xs, xr, hs, hr, ags, agr, *it = it
+    qs, qr, ds, dr, fxs, fxr, fgs, fgr, ffs, ffr = it
 
     row, col, dep = lax.axis_index("row"), lax.axis_index("col"), lax.axis_index("depth")
     y, k = row // 2, row % 2
@@ -83,6 +93,11 @@
     near = [at_y(1), at_y(2), at_y(3), at_x(1), at_x(2), at_x(3), other, up_z, down_z]
     for dev in near:
         pl.semaphore_signal(barrier, inc=1, device_id=dev, device_id_type=MESH)
+
+    left = dep < NZ // 2
+    rank = jnp.where(left, dep, NZ - 1 - dep)
+    inward = (row, col, jnp.where(left, dep + 1, dep - 1))
+    blk = k * NY + y
 
     def tell():
         pl.semaphore_signal(ring, inc=1, device_id=up_z, device_id_type=MESH)
@@ -138,12 +153,11 @@
             y_copy(s, o).start()
 
     def gather_copy(s, o):
-        blk = k * NY + y
         return copy(dbuf[s].at[blk], dbuf[s].at[blk], gs.at[s, o - 1], gr.at[s, o - 1], at_y(o))
 
     def cross_copy(s, o):
-        blk = k * NY + (y - o + NY) % NY
-        return copy(dbuf[s].at[blk], dbuf[s].at[blk], fs.at[s, o], fr.at[s, o], other)
+        b = k * NY + (y - o + NY) % NY
+        return copy(dbuf[s].at[b], dbuf[s].at[b], fs.at[s, o], fr.at[s, o], other)
 
     def middle(s):
         for o in (1, 2, 3):
@@ -155,7 +169,6 @@
             for o in range(3):
                 total = total + yrecv[s][o, m].astype(F32)
             sums.append(total)
-        blk = k * NY + y
         for m, value in enumerate(swiglu_back(*sums)):
             dbuf[s][blk, m] = value
         for o in (2, 1, 3):
@@ -203,52 +216,169 @@
     def z_down(u, j):
         return copy(zterm.at[u, j], zr.at[u, j], zs.at[u, j], zrr.at[u, j], down_z)
 
-    def place(q):
-        late = q - EARLY * HOPS
-        u = jnp.where(late < 0, q // HOPS, EARLY + late % LATE)
-        return u, jnp.where(late < 0, q % HOPS, late // LATE)
-
     def z_first(lo, hi):
         def send(q, carry):
-            u, j = place(q)
+            _, u, n = place(q, False)
 
             @pl.when(dep == 0)
             def _():
-                z_up(u, HOPS - j).start()
+                z_up(u, HOPS - n).start()
 
             @pl.when(dep == NZ - 1)
             def _():
-                z_down(u, j).start()
+                z_down(u, n).start()
 
             return carry
 
-        lax.fori_loop(lo * HOPS, hi * HOPS, send, 0)
+        lax.fori_loop(lo, hi, send, 0)
+
+    def forward_up(u, j, waits):
+        @pl.when(waits)
+        def _():
+            z_up(u, j).wait_recv()
+            zterm[u, j] = (zterm[u, j].astype(F32) + zl[u, j].astype(F32)).astype(BF)
+
+        z_up(u, j).start()
+
+    def forward_down(u, j, waits):
+        @pl.when(waits)
+        def _():
+            z_down(u, j).wait_recv()
+            zterm[u, j] = (zterm[u, j].astype(F32) + zr[u, j].astype(F32)).astype(BF)
+
+        z_down(u, j).start()
+
+    def place(q, far):
+        late = far & (q >= THIRD)
+        r2, r3 = jnp.maximum(q - SECOND, 0), jnp.maximum(q - THIRD, 0)
+        u = jnp.where(late, EARLY + r3 % LATE, 1 + r3 % (EARLY - 1))
+        u = jnp.where(q < THIRD, 2 + r2 % (EARLY - 2), u)
+        u = jnp.where(q < SECOND, jnp.where(q < FIRST, 0, 1), u)
+        n = jnp.where(late, r3 // LATE, FAR + r3 // (EARLY - 1))
+        n = jnp.where(q < THIRD, r2 // (EARLY - 2), n)
+        n = jnp.where(q < SECOND, jnp.where(q < FIRST, q, q - FIRST), n)
+        return late, u, n
 
     def z_step(t, carry):
         q = t - SKEW * (dep - 1)
-        u, j = place(jnp.clip(q, 0, STEPS - 1))
+        end = jnp.where(dep >= 2, FAR_STEPS, NEAR_STEPS)
+        late, u, j = place(jnp.clip(q, 0, end - 1), dep >= 2)
         j = HOPS - j
 
-        @pl.when((q >= 0) & (q < STEPS) & (j > dep) & (dep > 0))
-        def _():
-            z_up(u, j).wait_recv()
-            zterm[u, j] = (zterm[u, j].astype(F32) + zl[u, j].astype(F32)).astype(BF)
-            z_up(u, j).start()
+        @pl.when((q >= 0) & (q < end) & (j > dep) & (dep > 0))
+        def _():
+            forward_up(u, j, dep > jnp.where(late, 2, 0))
 
         p = t - SKEW * (NZ - 2 - dep)
-        v, i = place(jnp.clip(p, 0, STEPS - 1))
-
-        @pl.when((p >= 0) & (p < STEPS) & (i < dep) & (dep < NZ - 1))
-        def _():
-            z_down(v, i).wait_recv()
-            zterm[v, i] = (zterm[v, i].astype(F32) + zr[v, i].astype(F32)).astype(BF)
-            z_down(v, i).start()
+        end = jnp.where(dep <= NZ - 3, FAR_STEPS, NEAR_STEPS)
+        late, v, i = place(jnp.clip(p, 0, end - 1), dep <= NZ - 3)
+
+        @pl.when((p >= 0) & (p < end) & (i < dep) & (dep < NZ - 1))
+        def _():
+            forward_down(v, i, dep < jnp.where(late, NZ - 3, NZ - 1))
 
         return carry
 
     def z_steps(lo, hi):
         lax.fori_loop(lo, hi, z_step, 0)
 
+    def q_copy(slot, src):
+        return copy(src, fq.at[slot, x], qs.at[slot], qr.at[slot], inward)
+
+    def d_copy(n, slot, src):
+        return copy(src, fd[n].at[slot, blk], ds.at[n, slot], dr.at[n, slot], inward)
+
+    def fx_copy(slot, o):
+        return copy(fq.at[slot, x], fq.at[slot, x], fxs.at[slot, o - 1], fxr.at[slot, o - 1], at_x(o))
+
+    def fg_copy(n, slot, o):
+        return copy(
+            fd[n].at[slot, blk], fd[n].at[slot, blk], fgs.at[n, slot, o - 1], fgr.at[n, slot, o - 1], at_y(o)
+        )
+
+    def ff_copy(n, slot, o):
+        b = k * NY + (y - o + NY) % NY
+        return copy(fd[n].at[slot, b], fd[n].at[slot, b], ffs.at[n, slot, o], ffr.at[n, slot, o], other)
+
+    def send_q():
+        @pl.when(rank < 2)
+        def _():
+            part = pl.ds(pl.multiple_of(x * XTOK, XTOK), XTOK)
+            ownq[0] = x_ref[part, :]
+            ownq[1] = g_ref[part, :]
+            q_copy(rank, ownq).start()
+
+    def relay_q():
+        @pl.when(rank == 1)
+        def _():
+            q_copy(0, fq.at[0, x]).wait_recv()
+            q_copy(0, fq.at[0, x]).start()
+
+    def collect_q(slot):
+        @pl.when(rank == 2)
+        def _():
+            q_copy(slot, ownq).wait_recv()
+            for o in (2, 1, 3):
+                fx_copy(slot, o).start()
+
+    def turn_q(slot):
+        @pl.when(rank == 2)
+        def _():
+            for o in (1, 3, 2):
+                fx_copy(slot, o).wait_recv()
+            for m in range(2):
+                xt2[slot, m] = fq[slot, :, m].reshape(TOK, FEAT).T
+
+    def send_d(n):
+        @pl.when(rank < 2)
+        def _():
+            d_copy(n, rank, dbuf[MOVED[n]].at[blk]).start()
+
+    def relay_d(n):
+        @pl.when(rank == 1)
+        def _():
+            d_copy(n, 0, fd[n].at[0, blk]).wait_recv()
+            d_copy(n, 0, fd[n].at[0, blk]).start()
+
+    def collect_d(n, slot):
+        @pl.when(rank == 2)
+        def _():
+            d_copy(n, slot, fd[n].at[slot, blk]).wait_recv()
+            for o in (2, 1, 3):
+                fg_copy(n, slot, o).start()
+            ff_copy(n, slot, 0).start()
+
+    def spread_d(n, slot):
+        @pl.when(rank == 2)
+        def _():
+            for o in (1, 3, 2):
+                fg_copy(n, slot, o).wait_recv()
+                ff_copy(n, slot, o).start()
+
+    def add_d(n):
+        @pl.when(rank == 2)
+        def _():
+            lo, w = SLICES[MOVED[n]]
+            for slot in range(2):
+                for o in range(NY):
+                    ff_copy(n, slot, o).wait_recv()
+                for m in range(3):
+                    term = dot(xt2[slot, m // 2], fd[n][slot, :, m].reshape(TOK, w)) * factor
+                    for j in range(NZ):
+                        counts = jnp.where(left, j, NZ - 1 - j) > slot
+                        for v in range(w // LANE):
+                            u = lo // LANE + v
+                            rows = slice(m * CHUNK, (m + 1) * CHUNK)
+                            more = term[j * CHUNK:(j + 1) * CHUNK, v * LANE:(v + 1) * LANE]
+                            fsum[u - EARLY, j, rows, :] = (
+                                fsum[u - EARLY, j, rows, :] + jnp.where(counts, more, 0.0)
+                                if slot else jnp.where(counts, more, 0.0)
+                            )
+                            if slot:
+                                zterm[u, j, rows, :] = (
+                                    zterm[u, j, rows, :].astype(F32) + fsum[u - EARLY, j, rows, :]
+                                ).astype(BF)
+
     def x_copy(o):
         return copy(xsend.at[(x + o) % NX], xrecv.at[o - 1], xs.at[o - 1], xr.at[o - 1], at_x(o))
 
@@ -259,6 +389,7 @@
         return copy(agbuf.at[x], agbuf.at[x], ags.at[o - 1], agr.at[o - 1], at_x(o))
 
     first(0)
+    send_q()
     first(1)
     reduce_core(0)
     xt[0] = x_ref[...].T
@@ -270,10 +401,12 @@
     pass_on()
     first(3)
     reduce_core(2)
+    relay_q()
     spread(0)
     arrive(0)
     weights(0)
-    z_first(0, 1)
+    z_first(0, FIRST)
+    collect_q(1)
     pass_on()
     middle(1)
     reduce_core(3)
@@ -282,28 +415,36 @@
     spread(1)
     arrive(1)
     weights(1)
-    z_first(1, EARLY)
+    z_first(FIRST, SECOND)
+    collect_q(0)
     pass_on()
     middle(2)
     inputs(1)
     z_steps(0, 4)
     pass_on()
     middle(3)
-    z_steps(4, 7)
+    send_d(0)
     spread(2)
     arrive(2)
+    weights(2)
+    z_first(SECOND, NEAR_STEPS)
+    relay_d(0)
     inputs(2)
     pass_on()
-    z_steps(7, 10)
+    z_steps(4, 8)
     spread(3)
     arrive(3)
     inputs(3)
     for o in (2, 1, 3):
         x_copy(o).start()
-    weights(2)
+    collect_d(0, 1)
+    collect_d(0, 0)
     weights(3)
-    z_first(EARLY, UNITS)
-    z_steps(10, 20)
+    turn_q(1)
+    turn_q(0)
+    z_steps(8, 16)
+    spread_d(0, 1)
+    spread_d(0, 0)
     for o in (1, 3, 2):
         x_copy(o).wait_recv()
     mine = pl.ds(pl.multiple_of(x * XTOK, XTOK), XTOK)
@@ -313,7 +454,9 @@
     hsend[...] = total.astype(BF)
     pl.semaphore_wait(ring, 1)
     hi_copy().start()
-    z_steps(20, 36)
+    z_steps(16, THIRD + SKEW)
+    add_d(0)
+    z_steps(THIRD + SKEW, 36)
     hi_copy().wait_recv()
     agbuf[x] = (hsend[...].astype(F32) + hrecv[...].astype(F32)).astype(BF)
     for o in (2, 1, 3):
@@ -321,23 +464,20 @@
     z_steps(36, LAST)
 
     def finish(u, carry):
-        @pl.when(dep > 0)
-        def _():
-            z_up(u, dep).wait_recv()
-
-        @pl.when(dep < NZ - 1)
-        def _():
-            z_down(u, dep).wait_recv()
-
+        early = u < EARLY
+        from_below = dep > jnp.where(early, 0, 2)
+        from_above = dep < jnp.where(early, NZ - 1, NZ - 3)
         lanes = pl.ds(pl.multiple_of(u * LANE, LANE), LANE)
         wgr_ref[:, lanes] = zterm[u, dep].astype(F32)
 
-        @pl.when(dep > 0)
-        def _():
+        @pl.when(from_below)
+        def _():
+            z_up(u, dep).wait_recv()
             wgr_ref[:, lanes] += zl[u, dep].astype(F32)
 
-        @pl.when(dep < NZ - 1)
-        def _():
+        @pl.when(from_above)
+        def _():
+            z_down(u, dep).wait_recv()
             wgr_ref[:, lanes] += zr[u, dep].astype(F32)
 
         return carry
@@ -360,16 +500,47 @@
         ag_copy(o).wait_send()
     hi_copy().wait_send()
 
+    @pl.when(rank < 2)
+    def _():
+        q_copy(rank, ownq).wait_send()
+        for n in range(NM):
+            d_copy(n, rank, dbuf[MOVED[n]].at[blk]).wait_send()
+
+    @pl.when(rank == 1)
+    def _():
+        q_copy(0, ownq).wait_send()
+        for n in range(NM):
+            d_copy(n, 0, fd[n].at[0, blk]).wait_send()
+
+    @pl.when(rank == 2)
+    def _():
+        for slot in range(2):
+            for o in (1, 2, 3):
+                fx_copy(slot, o).wait_send()
+                for n in range(NM):
+                    fg_copy(n, slot, o).wait_send()
+            for o in range(NY):
+                for n in range(NM):
+                    ff_copy(n, slot, o).wait_send()
+
     def drain(q, carry):
         u, j = q // NZ, q % NZ
-
-        @pl.when(j != dep)
+        sends = ((j > dep) & (dep >= 2)) | ((j < dep) & (dep <= NZ - 3)) | ((j != dep) & (u < EARLY))
+
+        @pl.when(sends)
         def _():
             z_up(u, j).wait_send()
 
         return carry
 
     lax.fori_loop(0, UNITS * NZ, drain, 0)
+
+
+def results(ig_ref, wgr_ref, input_ref, gate_ref, up_ref, down_ref):
+    input_ref[...] = ig_ref[...].astype(F32)
+    gate_ref[...] = wgr_ref[:CHUNK]
+    up_ref[...] = wgr_ref[CHUNK:2 * CHUNK]
+    down_ref[...] = wgr_ref[2 * CHUNK:]
 
 
 def shards(layer_input, output_grad, w_gate, w_up, w_down):
@@ -403,6 +574,11 @@
         pltpu.VMEM((XTOK, FEAT), BF),
         pltpu.VMEM((XTOK, FEAT), BF),
         pltpu.VMEM((NX, XTOK, FEAT), BF),
+        pltpu.VMEM((2, XTOK, FEAT), BF),
+        pltpu.VMEM((2, NX, 2, XTOK, FEAT), BF),
+        pltpu.VMEM((2, 2, FEAT, TOK), BF),
+        pltpu.VMEM((LATE, NZ, ROWS, LANE), F32),
+        *[pltpu.VMEM((2, 2 * NY, 3, QUART, SLICES[s][1]), BF) for s in MOVED],
         dma((NS,)), dma((NS,)),
         dma((NS, 3)), dma((NS, 3)),
         dma((NS, 3)), dma((NS, 3)),
@@ -411,6 +587,11 @@
         dma((3,)), dma((3,)),
         dma((1,)), dma((1,)),
         dma((3,)), dma((3,)),
+        dma((2,)), dma((2,)),
+        dma((NM, 2)), dma((NM, 2)),
+        dma((2, 3)), dma((2, 3)),
+        dma((NM, 2, 3)), dma((NM, 2, 3)),
+        dma((NM, 2, NY)), dma((NM, 2, NY)),
     ]
     vmem = pl.BlockSpec(memory_space=pltpu.VMEM)
     ig, wgr = pl.pallas_call(
@@ -427,7 +608,19 @@
         ),
         name="swiglu_back",
     )(layer_input, output_grad, w_gate, w_up, w_down)
-    return ig.astype(F32), wgr[:CHUNK], wgr[CHUNK:2 * CHUNK], wgr[2 * CHUNK:].T
+    input_grad, gate_grad, up_grad, down_grad = pl.pallas_call(
+        results,
+        out_shape=(
+            jax.ShapeDtypeStruct((TOK, FEAT), F32),
+            jax.ShapeDtypeStruct((CHUNK, HID), F32),
+            jax.ShapeDtypeStruct((CHUNK, HID), F32),
+            jax.ShapeDtypeStruct((CHUNK, HID), F32),
+        ),
+        in_specs=[vmem] * 2,
+        out_specs=(vmem,) * 4,
+        name="results",
+    )(ig, wgr)
+    return input_grad, gate_grad, up_grad, down_grad.T
 
 
 def solution(mesh):

time: 134 us -> 120 us (0.90); the launches traced: 133 us -> 120 us
  Pallas kernels: 129 us -> 120 us
  local copies, waits for them, and re-layouts: 2.12 us -> 0 us
    pallas_call x1, Pallas kernels: 129 us -> 117 us  [shards(): pl.pallas_call(lambda *refs: kernel(factor, *refs), out_shape=(jax.ShapeD...]
    pallas_call x0 -> x1, Pallas kernels: none -> 2.72 us  [shards(): pl.pallas_call(results, out_shape=(jax.ShapeDtypeStruct((TOK, FEAT), F32)...]
    transpose x1 -> x0, local copies, waits for them, and re-layouts: 2.12 us -> none  [shards(): wgr[2 * CHUNK:]]
where the time goes in v3:
time: 120 us
  Pallas kernels  120 us (100%)
    pallas_call x1, Pallas kernels, shards(): pl.pallas_call(lambda *refs: kernel(factor, *refs), out_shape=(jax.ShapeD...  117 us
    pallas_call x1, Pallas kernels, shards(): pl.pallas_call(results, out_shape=(jax.ShapeDtypeStruct((TOK, FEAT), F32)...  2.72 us

profile of v3, /device:TPU:24, one launch (start us, length us, event | category | flops | bytes accessed | tf_op | source)
XLA Modules:
  0.0 120.1 jit_solution(16738537466718250802)
XLA Ops:
  0.6 116.8 %swiglu_back.1 = (bf16[512,640]{1,0:T(8,128)(2,1)}, f32[240,896]{1,0:T(8,128)}) custom-call(bf16[512,640]{1,0:T(8,128)(2,1)} %refs_0_.1, bf16[512,640]{1,0:T(8,128)(2,1)} %refs_1_.1, bf16[640,896]{1,0:T(8,128)(2,1)} %refs_2_.1, bf16[640,896]{1,0:T(8,128)(2,1)} %refs_3_.1, bf16[896,640]{1,0:T(8,128)(2,1)} %refs_4_.1), custom_call_target="tpu_custom_call" | custom-call | tf_op jit(solution)/shard_map/swiglu_back/pallas_call | solution.py:597
  117.4 2.7 %results.1 = (f32[512,640]{1,0:T(8,128)}, f32[80,896]{1,0:T(8,128)}, f32[80,896]{1,0:T(8,128)}, f32[80,896]{1,0:T(8,128)}) custom-call(bf16[512,640]{1,0:T(8,128)(2,1)} %get-tuple-element.10.ig_ref, f32[240,896]{1,0:T(8,128)} %get-tuple-element.11.wgr_ref), custom_call_target="tpu_custom_call" | custom-call | tf_op jit(solution)/shard_map/results/pallas_call | solution.py:611

commit v4 on v3

--- a/solution.py
+++ b/solution.py
@@ -25,6 +25,8 @@
 MOVED = (3,)
 NM = len(MOVED)
 SKEW = 4
+PIECES = 4
+PTOK = XTOK // PIECES
 FAR = HOPS - 2
 FIRST = HOPS
 SECOND = FIRST + FAR
@@ -382,11 +384,28 @@
     def x_copy(o):
         return copy(xsend.at[(x + o) % NX], xrecv.at[o - 1], xs.at[o - 1], xr.at[o - 1], at_x(o))
 
-    def hi_copy():
-        return copy(hsend, hrecv, hs.at[0], hr.at[0], partner)
-
-    def ag_copy(o):
-        return copy(agbuf.at[x], agbuf.at[x], ags.at[o - 1], agr.at[o - 1], at_x(o))
+    def hi_copy(n):
+        return copy(hsend.at[n], hrecv.at[n], hs.at[n], hr.at[n], partner)
+
+    def ag_copy(n, o):
+        return copy(agbuf.at[x, n], agbuf.at[x, n], ags.at[n, o - 1], agr.at[n, o - 1], at_x(o))
+
+    def sum_x():
+        for o in (1, 3, 2):
+            x_copy(o).wait_recv()
+        mine = pl.ds(pl.multiple_of(x * XTOK, XTOK), XTOK)
+        total = ig[mine, :]
+        for o in range(3):
+            total = total + xrecv[o].astype(F32)
+        for n in range(PIECES):
+            hsend[n] = total[n * PTOK:(n + 1) * PTOK].astype(BF)
+        pl.semaphore_wait(ring, 1)
+
+    def gather_x(n):
+        hi_copy(n).wait_recv()
+        agbuf[x, n] = (hsend[n].astype(F32) + hrecv[n].astype(F32)).astype(BF)
+        for o in (2, 1, 3):
+            ag_copy(n, o).start()
 
     first(0)
     send_q()
@@ -432,36 +451,37 @@
     inputs(2)
     pass_on()
     z_steps(4, 8)
+    collect_d(0, 1)
     spread(3)
     arrive(3)
+    collect_d(0, 0)
     inputs(3)
     for o in (2, 1, 3):
         x_copy(o).start()
-    collect_d(0, 1)
-    collect_d(0, 0)
     weights(3)
     turn_q(1)
     turn_q(0)
-    z_steps(8, 16)
+    z_steps(8, 14)
+    sum_x()
+    hi_copy(0).start()
+    z_steps(14, 17)
+    hi_copy(1).start()
     spread_d(0, 1)
     spread_d(0, 0)
-    for o in (1, 3, 2):
-        x_copy(o).wait_recv()
-    mine = pl.ds(pl.multiple_of(x * XTOK, XTOK), XTOK)
-    total = ig[mine, :]
-    for o in range(3):
-        total = total + xrecv[o].astype(F32)
-    hsend[...] = total.astype(BF)
-    pl.semaphore_wait(ring, 1)
-    hi_copy().start()
-    z_steps(16, THIRD + SKEW)
+    z_steps(17, 21)
+    hi_copy(2).start()
+    z_steps(21, THIRD + SKEW)
+    hi_copy(3).start()
     add_d(0)
-    z_steps(THIRD + SKEW, 36)
-    hi_copy().wait_recv()
-    agbuf[x] = (hsend[...].astype(F32) + hrecv[...].astype(F32)).astype(BF)
-    for o in (2, 1, 3):
-        ag_copy(o).start()
-    z_steps(36, LAST)
+    z_steps(THIRD + SKEW, 30)
+    gather_x(0)
+    z_steps(30, 33)
+    gather_x(1)
+    z_steps(33, 36)
+    gather_x(2)
+    z_steps(36, 39)
+    gather_x(3)
+    z_steps(39, 41)
 
     def finish(u, carry):
         early = u < EARLY
@@ -482,11 +502,7 @@
 
         return carry
 
-    lax.fori_loop(0, UNITS, finish, 0)
-
-    for o in (1, 3, 2):
-        ag_copy(o).wait_recv()
-    ig_ref[...] = agbuf[...].reshape(TOK, FEAT)
+    lax.fori_loop(0, EARLY, finish, 0)
 
     for s in range(NS):
         core_copy(s).wait_send()
@@ -497,8 +513,8 @@
             cross_copy(s, o).wait_send()
     for o in (1, 2, 3):
         x_copy(o).wait_send()
-        ag_copy(o).wait_send()
-    hi_copy().wait_send()
+    for n in range(PIECES):
+        hi_copy(n).wait_send()
 
     @pl.when(rank < 2)
     def _():
@@ -523,6 +539,17 @@
                 for n in range(NM):
                     ff_copy(n, slot, o).wait_send()
 
+    z_steps(41, LAST)
+    for n in range(PIECES):
+        for o in (1, 3, 2):
+            ag_copy(n, o).wait_recv()
+    out = pltpu.make_async_copy(agbuf, ig_ref, loads.at[0])
+    out.start()
+    lax.fori_loop(EARLY, UNITS, finish, 0)
+    for n in range(PIECES):
+        for o in (1, 2, 3):
+            ag_copy(n, o).wait_send()
+
     def drain(q, carry):
         u, j = q // NZ, q % NZ
         sends = ((j > dep) & (dep >= 2)) | ((j < dep) & (dep <= NZ - 3)) | ((j != dep) & (u < EARLY))
@@ -534,6 +561,7 @@
         return carry
 
     lax.fori_loop(0, UNITS * NZ, drain, 0)
+    out.wait()
 
 
 def results(ig_ref, wgr_ref, input_ref, gate_ref, up_ref, down_ref):
@@ -571,9 +599,9 @@
         pltpu.VMEM((TOK, FEAT), F32),
         pltpu.VMEM((NX, XTOK, FEAT), BF),
         pltpu.VMEM((NX - 1, XTOK, FEAT), BF),
-        pltpu.VMEM((XTOK, FEAT), BF),
-        pltpu.VMEM((XTOK, FEAT), BF),
-        pltpu.VMEM((NX, XTOK, FEAT), BF),
+        pltpu.VMEM((PIECES, PTOK, FEAT), BF),
+        pltpu.VMEM((PIECES, PTOK, FEAT), BF),
+        pltpu.VMEM((NX, PIECES, PTOK, FEAT), BF),
         pltpu.VMEM((2, XTOK, FEAT), BF),
         pltpu.VMEM((2, NX, 2, XTOK, FEAT), BF),
         pltpu.VMEM((2, 2, FEAT, TOK), BF),
@@ -585,8 +613,8 @@
         dma((NS, NY)), dma((NS, NY)),
         dma((UNITS, NZ)), dma((UNITS, NZ)), dma((UNITS, NZ)),
         dma((3,)), dma((3,)),
-        dma((1,)), dma((1,)),
-        dma((3,)), dma((3,)),
+        dma((PIECES,)), dma((PIECES,)),
+        dma((PIECES, 3)), dma((PIECES, 3)),
         dma((2,)), dma((2,)),
         dma((NM, 2)), dma((NM, 2)),
         dma((2, 3)), dma((2, 3)),
@@ -597,11 +625,11 @@
     ig, wgr = pl.pallas_call(
         lambda *refs: kernel(factor, *refs),
         out_shape=(
-            jax.ShapeDtypeStruct((TOK, FEAT), BF),
+            jax.ShapeDtypeStruct((NX, PIECES, PTOK, FEAT), BF),
             jax.ShapeDtypeStruct((ROWS, HID), F32),
         ),
         in_specs=[pl.BlockSpec(memory_space=pl.ANY)] * 5,
-        out_specs=(vmem, vmem),
+        out_specs=(pl.BlockSpec(memory_space=pl.ANY), vmem),
         scratch_shapes=scratch,
         compiler_params=pltpu.CompilerParams(
             collective_id=0, has_side_effects=True, vmem_limit_bytes=56 * 2 ** 20
@@ -619,7 +647,7 @@
         in_specs=[vmem] * 2,
         out_specs=(vmem,) * 4,
         name="results",
-    )(ig, wgr)
+    )(ig.reshape(TOK, FEAT), wgr)
     return input_grad, gate_grad, up_grad, down_grad.T
 
 

time: 120 us -> 122 us (1.017)
  Pallas kernels: 120 us -> 122 us
    pallas_call x1, Pallas kernels: 117 us -> 119 us  [shards(): pl.pallas_call(lambda *refs: kernel(factor, *refs), out_shape=(jax.ShapeD...]
where the time goes in v4:
time: 122 us
  Pallas kernels  122 us (100%)
    pallas_call x1, Pallas kernels, shards(): pl.pallas_call(lambda *refs: kernel(factor, *refs), out_shape=(jax.ShapeD...  119 us
    pallas_call x1, Pallas kernels, shards(): pl.pallas_call(results, out_shape=(jax.ShapeDtypeStruct((TOK, FEAT), F32)...  2.72 us

profile of v4, /device:TPU:24, one launch (start us, length us, event | category | flops | bytes accessed | tf_op | source)
XLA Modules:
  0.0 122.2 jit_solution(844235110239859194)
XLA Ops:
  0.6 118.9 %swiglu_back.1 = (bf16[4,4,32,640]{3,2,1,0:T(8,128)(2,1)}, f32[240,896]{1,0:T(8,128)}) custom-call(bf16[512,640]{1,0:T(8,128)(2,1)} %refs_0_.1, bf16[512,640]{1,0:T(8,128)(2,1)} %refs_1_.1, bf16[640,896]{1,0:T(8,128)(2,1)} %refs_2_.1, bf16[640,896]{1,0:T(8,128)(2,1)} %refs_3_.1, bf16[896,640]{1,0:T(8,128)(2,1)} %refs_4_.1), custom_call_target="tpu_custom_call" | custom-call | tf_op jit(solution)/shard_map/swiglu_back/pallas_call | solution.py:625
  119.5 2.7 %results.1 = (f32[512,640]{1,0:T(8,128)}, f32[80,896]{1,0:T(8,128)}, f32[80,896]{1,0:T(8,128)}, f32[80,896]{1,0:T(8,128)}) custom-call(bf16[512,640]{1,0:T(8,128)(2,1)} %bitcast.2, f32[240,896]{1,0:T(8,128)} %get-tuple-element.11.wgr_ref), custom_call_target="tpu_custom_call" | custom-call | tf_op jit(solution)/shard_map/results/pallas_call | solution.py:639

commit v5 on v4

--- a/solution.py
+++ b/solution.py
@@ -451,13 +451,13 @@
     inputs(2)
     pass_on()
     z_steps(4, 8)
-    collect_d(0, 1)
     spread(3)
     arrive(3)
-    collect_d(0, 0)
     inputs(3)
     for o in (2, 1, 3):
         x_copy(o).start()
+    collect_d(0, 1)
+    collect_d(0, 0)
     weights(3)
     turn_q(1)
     turn_q(0)

time: 122 us -> 120 us (0.984)
  Pallas kernels: 122 us -> 119 us
    pallas_call x1, Pallas kernels: 119 us -> 117 us  [shards(): pl.pallas_call(lambda *refs: kernel(factor, *refs), out_shape=(jax.ShapeD...]
where the time goes in v5:
time: 120 us
  Pallas kernels  119 us (99%)
    pallas_call x1, Pallas kernels, shards(): pl.pallas_call(lambda *refs: kernel(factor, *refs), out_shape=(jax.ShapeD...  117 us
    pallas_call x1, Pallas kernels, shards(): pl.pallas_call(results, out_shape=(jax.ShapeDtypeStruct((TOK, FEAT), F32)...  2.72 us

profile of v5, /device:TPU:24, one launch (start us, length us, event | category | flops | bytes accessed | tf_op | source)
XLA Modules:
  0.0 120.0 jit_solution(6346331376444150201)
XLA Ops:
  0.6 116.7 %swiglu_back.1 = (bf16[4,4,32,640]{3,2,1,0:T(8,128)(2,1)}, f32[240,896]{1,0:T(8,128)}) custom-call(bf16[512,640]{1,0:T(8,128)(2,1)} %refs_0_.1, bf16[512,640]{1,0:T(8,128)(2,1)} %refs_1_.1, bf16[640,896]{1,0:T(8,128)(2,1)} %refs_2_.1, bf16[640,896]{1,0:T(8,128)(2,1)} %refs_3_.1, bf16[896,640]{1,0:T(8,128)(2,1)} %refs_4_.1), custom_call_target="tpu_custom_call" | custom-call | tf_op jit(solution)/shard_map/swiglu_back/pallas_call | solution.py:625
  117.3 2.7 %results.1 = (f32[512,640]{1,0:T(8,128)}, f32[80,896]{1,0:T(8,128)}, f32[80,896]{1,0:T(8,128)}, f32[80,896]{1,0:T(8,128)}) custom-call(bf16[512,640]{1,0:T(8,128)(2,1)} %bitcast.2, f32[240,896]{1,0:T(8,128)} %get-tuple-element.11.wgr_ref), custom_call_target="tpu_custom_call" | custom-call | tf_op jit(solution)/shard_map/results/pallas_call | solution.py:639
